TPU v7x, 32 devices: a whole 2x2x4 slice. The times are simulated.
32 devices in a mesh: ctx: 8 (over z, core), fsdp: 4 (over y, x).
Axes of the slice: x: 2, y: 2, z: 4, core: 2. Of those that a mesh axis runs over, the one named last changes fastest.
Arguments:
- inputs: bfloat16 [4, 4096, 1280], P('fsdp', 'ctx'), may hold values from -6 to 6
- cotangent: bfloat16 [4, 4096, 1280], P('fsdp', 'ctx'), may hold values from -6 to 6
- block_order: int32 [4, 16], P('fsdp'), may hold values from 0 to 15, each once within a row
- w_qkv: float32 [1280, 3840], P('fsdp'), may hold values from -0.15625 to 0.15625
- m_qkv: float32 [1280, 3840], P('fsdp'), may hold values from -768 to 768
- v_qkv: float32 [1280, 3840], P('fsdp'), may hold values from 16384 to 65536
- w_out: float32 [1280, 1280], P('fsdp'), may hold values from -2.5 to 2.5
- m_out: float32 [1280, 1280], P('fsdp'), may hold values from -64 to 64
- v_out: float32 [1280, 1280], P('fsdp'), may hold values from 124 to 496
- w_up: float32 [1280, 1280], P('fsdp'), may hold values from -0.15625 to 0.15625
- m_up: float32 [1280, 1280], P('fsdp'), may hold values from -384 to 384
- v_up: float32 [1280, 1280], P('fsdp'), may hold values from 4096 to 16384
- w_down: float32 [1280, 1280], P('fsdp'), may hold values from -0.15625 to 0.15625
- m_down: float32 [1280, 1280], P('fsdp'), may hold values from -448 to 448
- v_down: float32 [1280, 1280], P('fsdp'), may hold values from 5898.24 to 23592.96
- small_params: float32 [2640], replicated, may hold values from -1 to 2, as said below
- small_m: float32 [2640], replicated, may hold values from -576 to 576
- small_v: float32 [2640], replicated, may hold values from 4096 to 147456
Outputs:
- output: bfloat16 [4, 4096, 1280], P('fsdp', 'ctx')
- input_grad: bfloat16 [4, 4096, 1280], P('fsdp', 'ctx')
- qkv_new: float32 [1280, 3840], P('fsdp')
- qkv_first: float32 [1280, 3840], P('fsdp')
- qkv_second: float32 [1280, 3840], P('fsdp')
- qkv_low: bfloat16 [1280, 3840], P('fsdp')
- out_new: float32 [1280, 1280], P('fsdp')
- out_first: float32 [1280, 1280], P('fsdp')
- out_second: float32 [1280, 1280], P('fsdp')
- out_low: bfloat16 [1280, 1280], P('fsdp')
- up_new: float32 [1280, 1280], P('fsdp')
- up_first: float32 [1280, 1280], P('fsdp')
- up_second: float32 [1280, 1280], P('fsdp')
- up_low: bfloat16 [1280, 1280], P('fsdp')
- down_new: float32 [1280, 1280], P('fsdp')
- down_first: float32 [1280, 1280], P('fsdp')
- down_second: float32 [1280, 1280], P('fsdp')
- down_low: bfloat16 [1280, 1280], P('fsdp')
- small_new: float32 [2640], replicated
- small_first: float32 [2640], replicated
- small_second: float32 [2640], replicated
Inputs may be any that keep to these rules, and one draw needn't show every extreme that they name: `block_order`: each row lists the 16 causal blocks of its group once each. ctx index c holds the blocks at entries 2 c to 2 c + 1, in that order. Blocks below 8 form the prompt in order; block 8 + j is part (j % 2) of continuation j // 2. `small_params`: entries 0 to 2559 are gains; the last 80 are query scale parameters.
All inputs are finite; a program needn't handle non-finite values.
Results may differ from a plain program's by a relative error of at most 0.025.
Values may be sent and summed in bfloat16 or wider, within the bound.
A program may use at most 384 MiB of HBM per device.

v0:
```python
import functools
import math
import jax
import jax.numpy as jnp
from jax import lax
from jax.sharding import PartitionSpec as P

D = 1280
H = 16
HD = 80
FF = 1280
BLOCK = 256
CONT = 512
STEP = 3
norm_eps = 1e-06
beta_one = 0.5
beta_two = 0.5
adam_eps = 1e-08
decay_rate = 0.1
small_rate = 0.75
qkv_rate_base = 1.0
scale_base = 1.442695


def token_layout(block_ids):
    num_blocks = block_ids.shape[0]
    prompt_blocks = num_blocks // 2
    cont_blocks = CONT // BLOCK
    later = block_ids - prompt_blocks
    block_seg = jnp.where(block_ids < prompt_blocks, 0, 1 + later // cont_blocks)
    block_base = jnp.where(
        block_ids < prompt_blocks, block_ids * BLOCK, (prompt_blocks + later % cont_blocks) * BLOCK
    )
    offset = jnp.arange(BLOCK, dtype=jnp.int32)
    seg_ids = jnp.broadcast_to(block_seg[:, None], (num_blocks, BLOCK)).reshape(-1)
    positions = (block_base[:, None] + offset[None, :]).reshape(-1)
    return (seg_ids, positions)


def pair_mask(seg_query, pos_query, seg_key, pos_key):
    same_doc = (seg_key[None, :] == 0) | (seg_key[None, :] == seg_query[:, None])
    return (same_doc & (pos_key[None, :] <= pos_query[:, None]))[None]


def rms_scale(values):
    return lax.rsqrt(jnp.mean(values * values, axis=-1, keepdims=True) + norm_eps)


def head_scores(query_heads, key_heads):
    return jnp.einsum("qhd,khd->hqk", query_heads, key_heads, preferred_element_type=jnp.float32)


def adamw(weight, first, second, gradient, step_rate, decay_on):
    first_new = beta_one * first + (1.0 - beta_one) * gradient
    second_new = beta_two * second + (1.0 - beta_two) * gradient * gradient
    corr_one = 1.0 - beta_one**STEP
    corr_two = 1.0 - beta_two**STEP
    update = first_new / corr_one / (jnp.sqrt(second_new / corr_two) + adam_eps)
    weight_new = weight - step_rate * (update + decay_on * weight)
    return (weight_new, first_new, second_new)


def body(
    inputs,
    cotangent,
    block_order,
    w_qkv,
    m_qkv,
    v_qkv,
    w_out,
    m_out,
    v_out,
    w_up,
    m_up,
    v_up,
    w_down,
    m_down,
    v_down,
    small_params,
    small_m,
    small_v,
):
    rows_dev = inputs.shape[1]
    bf16 = jnp.bfloat16
    f32 = jnp.float32
    qkv_full, out_full, up_full, down_full = (
        lax.all_gather(w_qkv.astype(bf16), "fsdp", axis=0, tiled=True),
        lax.all_gather(w_out.astype(bf16), "fsdp", axis=0, tiled=True),
        lax.all_gather(w_up.astype(bf16), "fsdp", axis=0, tiled=True),
        lax.all_gather(w_down.astype(bf16), "fsdp", axis=0, tiled=True),
    )
    seg_all, pos_all = token_layout(block_order[0])
    here_row = lax.axis_index("ctx") * rows_dev
    seg_here = lax.dynamic_slice_in_dim(seg_all, here_row, rows_dev, 0)
    pos_here = lax.dynamic_slice_in_dim(pos_all, here_row, rows_dev, 0)
    gain_one = small_params[:D]
    gain_two = small_params[D : 2 * D]
    query_scale = small_params[2 * D :]
    layer_in = inputs[0].astype(f32)
    scale_one = rms_scale(layer_in)
    unit_one = layer_in * scale_one
    normed = (unit_one * gain_one).astype(bf16)
    qkv = jnp.dot(normed, qkv_full, preferred_element_type=f32)
    factor = scale_base / math.sqrt(HD) * jax.nn.softplus(query_scale)
    query_raw = qkv[:, :D].reshape(rows_dev, H, HD)
    queries = (query_raw * factor).astype(bf16)
    keys_here = qkv[:, D : 2 * D].astype(bf16)
    values_here = qkv[:, 2 * D :].astype(bf16)
    keys_all, values_all = (
        lax.all_gather(keys_here, "ctx", axis=0, tiled=True),
        lax.all_gather(values_here, "ctx", axis=0, tiled=True),
    )
    key_total = keys_all.shape[0]
    key_block = math.gcd(key_total, 512)
    num_blocks = key_total // key_block
    key_stack = (
        keys_all.reshape(num_blocks, key_block, H, HD),
        values_all.reshape(num_blocks, key_block, H, HD),
        seg_all.reshape(num_blocks, key_block),
        pos_all.reshape(num_blocks, key_block),
    )

    def stat_step(running, key_set):
        row_top, row_mass = running
        scores = head_scores(queries, key_set[0])
        allowed = pair_mask(seg_here, pos_here, key_set[2], key_set[3])
        block_top = jnp.max(jnp.where(allowed, scores, -1e30), axis=-1)
        new_top = jnp.maximum(row_top, block_top)
        row_mass = row_mass * jnp.exp(row_top - new_top) + jnp.sum(
            jnp.where(allowed, jnp.exp(scores - new_top[..., None]), 0.0), axis=-1
        )
        return ((new_top, row_mass), None)

    start_stats = (jnp.full((H, rows_dev), -1e30, f32), jnp.zeros((H, rows_dev), f32))
    (row_top, row_mass), unused = lax.scan(stat_step, start_stats, key_stack)
    row_lse = row_top + jnp.log(row_mass)

    def value_step(mixed_acc, key_set):
        scores = head_scores(queries, key_set[0])
        allowed = pair_mask(seg_here, pos_here, key_set[2], key_set[3])
        prob_rows = jnp.where(allowed, jnp.exp(scores - row_lse[..., None]), 0.0).astype(bf16)
        return (
            mixed_acc
            + jnp.einsum("hqk,khd->qhd", prob_rows, key_set[1], preferred_element_type=f32),
            None,
        )

    mixed, unused = lax.scan(value_step, jnp.zeros((rows_dev, H, HD), f32), key_stack)
    attn_low = mixed.reshape(rows_dev, D).astype(bf16)
    mid = layer_in + jnp.dot(attn_low, out_full, preferred_element_type=f32)
    scale_two = rms_scale(mid)
    unit_two = mid * scale_two
    normed_two = (unit_two * gain_two).astype(bf16)
    hidden = jnp.dot(normed_two, up_full, preferred_element_type=f32)
    gate_sig = jax.nn.sigmoid(hidden)
    act = (hidden * gate_sig).astype(bf16)
    output = (mid + jnp.dot(act, down_full, preferred_element_type=f32)).astype(bf16)
    grad_in = cotangent[0]
    grad_down = jnp.dot(act.T, grad_in, preferred_element_type=f32)
    dact = jnp.dot(grad_in, down_full.T, preferred_element_type=f32)
    dhidden = (dact * gate_sig * (1.0 + hidden * (1.0 - gate_sig))).astype(bf16)
    grad_up = jnp.dot(normed_two.T, dhidden, preferred_element_type=f32)
    dnormed_two = jnp.dot(dhidden, up_full.T, preferred_element_type=f32)
    dunit_two = dnormed_two * gain_two
    dmid = grad_in.astype(f32) + scale_two * (
        dunit_two - unit_two * jnp.mean(dunit_two * unit_two, axis=-1, keepdims=True)
    )
    gain_two_grad = jnp.sum(dnormed_two * unit_two, axis=0)
    dbranch = dmid.astype(bf16)
    grad_out = jnp.dot(attn_low.T, dbranch, preferred_element_type=f32)
    dattn = jnp.dot(dbranch, out_full.T, preferred_element_type=f32).astype(bf16)
    dattn_heads = dattn.reshape(rows_dev, H, HD)
    row_delta = jnp.sum(dattn_heads.astype(f32) * mixed, axis=-1).T

    def back_step(dq_acc, key_set, want_keys):
        scores = head_scores(queries, key_set[0])
        allowed = pair_mask(seg_here, pos_here, key_set[2], key_set[3])
        prob_rows = jnp.where(allowed, jnp.exp(scores - row_lse[..., None]), 0.0)
        grad_probs = jnp.einsum("qhd,khd->hqk", dattn_heads, key_set[1], preferred_element_type=f32)
        grad_scores = (prob_rows * (grad_probs - row_delta[..., None])).astype(bf16)
        dq_acc = dq_acc + jnp.einsum(
            "hqk,khd->qhd", grad_scores, key_set[0], preferred_element_type=f32
        )
        grad_keys = jnp.einsum("hqk,qhd->khd", grad_scores, queries, preferred_element_type=f32)
        grad_values = jnp.einsum(
            "hqk,qhd->khd", prob_rows.astype(bf16), dattn_heads, preferred_element_type=f32
        )
        return (dq_acc, (grad_keys.reshape(-1, D), grad_values.reshape(-1, D)))

    dq_start = jnp.zeros((rows_dev, H, HD), f32)
    dq_acc, key_parts = lax.scan(functools.partial(back_step, want_keys=True), dq_start, key_stack)
    dkeys_all = key_parts[0].reshape(key_total, D)
    dvalues_all = key_parts[1].reshape(key_total, D)
    dkeys_here, dvalues_here = (
        lax.psum_scatter(
            dkeys_all.astype(jnp.bfloat16), "ctx", scatter_dimension=0, tiled=True
        ).astype(jnp.float32),
        lax.psum_scatter(
            dvalues_all.astype(jnp.bfloat16), "ctx", scatter_dimension=0, tiled=True
        ).astype(jnp.float32),
    )
    dqkv = jnp.concatenate(
        [(dq_acc * factor).reshape(rows_dev, D), dkeys_here, dvalues_here], axis=1
    ).astype(bf16)
    scale_grad = (
        jnp.sum(dq_acc * query_raw, axis=(0, 1))
        * (scale_base / math.sqrt(HD))
        * jax.nn.sigmoid(query_scale)
    )
    grad_qkv = jnp.dot(normed.T, dqkv, preferred_element_type=f32)
    dnormed = jnp.dot(dqkv, qkv_full.T, preferred_element_type=f32)
    dunit_one = dnormed * gain_one
    input_grad = dmid + scale_one * (
        dunit_one - unit_one * jnp.mean(dunit_one * unit_one, axis=-1, keepdims=True)
    )
    gain_one_grad = jnp.sum(dnormed * unit_one, axis=0)
    small_grad = jnp.concatenate([gain_one_grad, gain_two_grad, scale_grad])
    small_total = lax.psum(small_grad, ("ctx", "fsdp"))
    rate_qkv = qkv_rate_base / math.sqrt(D)
    rate_out = 0.5 / math.sqrt(max(D // 256, 1))
    rate_up = 0.5 / math.sqrt(D)
    rate_down = 0.5 / math.sqrt(FF)
    shard_qkv, shard_out, shard_up, shard_down = (
        lax.psum_scatter(
            grad_qkv.astype(jnp.bfloat16), "fsdp", scatter_dimension=0, tiled=True
        ).astype(jnp.float32),
        lax.psum_scatter(
            grad_out.astype(jnp.bfloat16), "fsdp", scatter_dimension=0, tiled=True
        ).astype(jnp.float32),
        lax.psum_scatter(
            grad_up.astype(jnp.bfloat16), "fsdp", scatter_dimension=0, tiled=True
        ).astype(jnp.float32),
        lax.psum_scatter(
            grad_down.astype(jnp.bfloat16), "fsdp", scatter_dimension=0, tiled=True
        ).astype(jnp.float32),
    )
    total_qkv, total_out, total_up, total_down = (
        lax.psum(shard_qkv.astype(jnp.bfloat16), "ctx").astype(jnp.float32),
        lax.psum(shard_out.astype(jnp.bfloat16), "ctx").astype(jnp.float32),
        lax.psum(shard_up.astype(jnp.bfloat16), "ctx").astype(jnp.float32),
        lax.psum(shard_down.astype(jnp.bfloat16), "ctx").astype(jnp.float32),
    )
    qkv_set = adamw(w_qkv, m_qkv, v_qkv, total_qkv, rate_qkv, decay_rate)
    out_set = adamw(w_out, m_out, v_out, total_out, rate_out, decay_rate)
    up_set = adamw(w_up, m_up, v_up, total_up, rate_up, decay_rate)
    down_set = adamw(w_down, m_down, v_down, total_down, rate_down, decay_rate)
    small_set = adamw(small_params, small_m, small_v, small_total, small_rate, 0.0)
    return (
        output[None],
        input_grad.astype(bf16)[None],
        qkv_set[0],
        qkv_set[1],
        qkv_set[2],
        qkv_set[0].astype(bf16),
        out_set[0],
        out_set[1],
        out_set[2],
        out_set[0].astype(bf16),
        up_set[0],
        up_set[1],
        up_set[2],
        up_set[0].astype(bf16),
        down_set[0],
        down_set[1],
        down_set[2],
        down_set[0].astype(bf16),
        small_set[0],
        small_set[1],
        small_set[2],
    )


def solution(mesh):
    in_specs = (
        P("fsdp", "ctx", None),
        P("fsdp", "ctx", None),
        P("fsdp", None),
        P("fsdp", None),
        P("fsdp", None),
        P("fsdp", None),
        P("fsdp", None),
        P("fsdp", None),
        P("fsdp", None),
        P("fsdp", None),
        P("fsdp", None),
        P("fsdp", None),
        P("fsdp", None),
        P("fsdp", None),
        P("fsdp", None),
        P(),
        P(),
        P(),
    )
    out_specs = (
        P("fsdp", "ctx", None),
        P("fsdp", "ctx", None),
        P("fsdp", None),
        P("fsdp", None),
        P("fsdp", None),
        P("fsdp", None),
        P("fsdp", None),
        P("fsdp", None),
        P("fsdp", None),
        P("fsdp", None),
        P("fsdp", None),
        P("fsdp", None),
        P("fsdp", None),
        P("fsdp", None),
        P("fsdp", None),
        P("fsdp", None),
        P("fsdp", None),
        P("fsdp", None),
        P(),
        P(),
        P(),
    )
    return jax.shard_map(body, mesh=mesh, in_specs=in_specs, out_specs=out_specs, check_vma=False)
```

profile of v0, /device:TPU:0, one launch (start us, length us, event | category | flops | bytes accessed | tf_op | source)
XLA Modules:
  0.0 1684.8 jit_solution(14041899212990422532)
XLA Ops:
  13.6 100.2 %all-gather.7.cloned.1.call-done = bf16[1280,3840]{1,0:T(8,128)(2,1)} async-done(((bf16[320,3840]{1,0:T(8,128)(2,1)}), bf16[1280,3840]{1,0:T(8,128)(2,1)}) %all-gather.7.cloned.1.call-update) | async-done | bytes 9830416 | tf_op jit(solution)/shard_map/all_gather | solution.py:87
  113.8 11.3 fusion.97
  143.0 83.4 %all-gather.11.cloned.1.call-done = bf16[4096,1280]{1,0:T(8,128)(2,1)} async-done(((bf16[512,1280]{1,0:T(8,128)(2,1)}), bf16[4096,1280]{1,0:T(8,128)(2,1)}) %all-gather.11.cloned.1.call-update) | async-done | bytes 10485776 | tf_op jit(solution)/shard_map/all_gather | solution.py:110
  226.4 14.5 copy.59
  240.9 15.1 copy.93
  256.0 16.3 copy.63
  272.3 11.7 copy.61
  284.0 42.4 %all-gather.9.cloned.1.call-done = bf16[4096,1280]{1,0:T(8,128)(2,1)} async-done(((bf16[512,1280]{1,0:T(8,128)(2,1)}), bf16[4096,1280]{1,0:T(8,128)(2,1)}) %all-gather.9.cloned.1.call-update) | async-done | bytes 10485776 | tf_op jit(solution)/shard_map/all_gather | solution.py:111
  326.4 29.8 %reshape.410 = bf16[8,512,16,80]{3,2,1,0:T(8,128)(2,1)} reshape(bf16[4096,1280]{1,0:T(8,128)(2,1)} %all-gather.9.cloned.1.call-done) | data formatting | bytes 20971520 | tf_op jit(solution)/shard_map/reshape | solution.py:118
  356.2 21.7 %copy.62 = bf16[8,512,16,80]{1,3,2,0:T(8,128)(2,1)} copy(bf16[8,512,16,80]{3,2,1,0:T(8,128)(2,1)} %reshape.410) | data formatting | bytes 20971520
  378.0 150.4 %while.39 = (s32[]{:T(128)}, f32[16,512]{1,0:T(8,128)S(1)}, f32[16,512]{1,0:T(8,128)S(1)}, s32[8,512]{1,0:T(8,128)S(1)}, s32[512]{0:T(512)S(1)}, /*index=5*/s32[...) while((s32[]{:T(128)}, f32[16,512]{1,0:T(8,128)S(1)}, ...), condition=%wide.region_4.5_spmd.clone, body=%wide.region_1.4_spmd.clone.sunk | while | flops 693150208 | bytes 37405832 | solution.py:135
  528.4 95.0 %while.40 = (s32[]{:T(128)}, f32[512,16,80]{0,2,1:T(8,128)}, bf16[8,512,16,80]{1,3,2,0:T(8,128)(2,1)}, s32[8,512]{1,0:T(8,128)S(1)}, s32[512]{0:T(512)S(1)}, /*i...) while((s32[]{:T(128)}, f32[512,16,80]{0,2,1:T(8,128)}, ...), condition=%wide.region_6.7_spmd.clone, body=%wide.region_5.6_spmd.clone.sunk | while | flops 1357120000 | bytes 13157527 | solution.py:148
  655.5 418.3 %while.41 = (s32[]{:T(128)}, f32[512,16,80]{0,2,1:T(8,128)}, bf16[8,512,1280]{2,1,0:T(8,128)(2,1)}, bf16[8,512,1280]{2,1,0:T(8,128)(2,1)}, bf16[8,512,16,80]{1,3...) while((s32[]{:T(128)}, f32[512,16,80]{0,2,1:T(8,128)}, ...), condition=%wide.region_11.12_spmd.clone, body=%wide.region_10.11_spmd.clone.sunk | while | flops 3391357440 | bytes 103924920 | solution.py:191
  665.3 11.1 fusion.157
  683.1 9.9 fusion.158
  717.0 11.1 fusion.157
  769.4 11.1 fusion.157
  821.8 11.1 fusion.157
  874.1 11.1 fusion.157
  926.4 11.1 fusion.157
  978.8 11.1 fusion.157
  1031.1 11.1 fusion.157
  1100.8 81.0 %reduce-scatter.9.cloned.1.call-done = bf16[512,1280]{1,0:T(8,128)(2,1)} async-done(((bf16[4096,1280]{1,0:T(8,128)(2,1)}), bf16[512,1280]{1,0:T(8,128)(2,1)}) %reduce-scatter.9.cloned.1.call-update) | async-done | bytes 1310736 | tf_op jit(solution)/shard_map/reduce_scatter | solution.py:198
  1181.9 110.1 %reduce-scatter.7.cloned.1.call-done = bf16[512,1280]{1,0:T(8,128)(2,1)} async-done(((bf16[4096,1280]{1,0:T(8,128)(2,1)}), bf16[512,1280]{1,0:T(8,128)(2,1)}) %reduce-scatter.7.cloned.1.call-update) | async-done | bytes 1310736 | tf_op jit(solution)/shard_map/reduce_scatter | solution.py:195
  1309.2 29.8 %reduce-scatter.13.cloned.1.call-done = bf16[320,1280]{1,0:T(8,128)(2,1)} async-done(((bf16[1280,1280]{1,0:T(8,128)(2,1)}), bf16[320,1280]{1,0:T(8,128)(2,1)}) %reduce-scatter.13.cloned.1.call-update) | async-done | bytes 819216 | tf_op jit(solution)/shard_map/reduce_scatter | solution.py:227
  1339.0 48.5 %reduce-scatter.15.cloned.1.call-done = bf16[320,1280]{1,0:T(8,128)(2,1)} async-done(((bf16[1280,1280]{1,0:T(8,128)(2,1)}), bf16[320,1280]{1,0:T(8,128)(2,1)}) %reduce-scatter.15.cloned.1.call-update) | async-done | bytes 819216 | tf_op jit(solution)/shard_map/reduce_scatter | solution.py:230
  1387.6 48.7 %reduce-scatter.17.cloned.1.call-done = bf16[320,1280]{1,0:T(8,128)(2,1)} async-done(((bf16[1280,1280]{1,0:T(8,128)(2,1)}), bf16[320,1280]{1,0:T(8,128)(2,1)}) %reduce-scatter.17.cloned.1.call-update) | async-done | bytes 819216 | tf_op jit(solution)/shard_map/reduce_scatter | solution.py:233
  1436.3 101.2 %reduce-scatter.11.cloned.1.call-done = bf16[320,3840]{1,0:T(8,128)(2,1)} async-done(((bf16[1280,3840]{1,0:T(8,128)(2,1)}), bf16[320,3840]{1,0:T(8,128)(2,1)}) %reduce-scatter.11.cloned.1.call-update) | async-done | bytes 2457616 | tf_op jit(solution)/shard_map/reduce_scatter | solution.py:224
  1537.6 10.9 fusion.56
  1548.5 41.0 %psum.39 = f32[2640]{0:T(1024)S(1)} all-reduce(f32[2640]{0:T(1024)S(1)} %pad_maximum_fusion.3), channel_id=1, replica_groups=mesh['ctx'=8,'fsdp'=4] {'ctx','fsdp'}, use_global_device_ids=true, to_apply=%region_26.27 | all-reduce | flops 2640 | bytes 21120 | tf_op jit(solution)/shard_map/psum | solution.py:218
  1594.4 57.9 %all-reduce.3.cloned.1.call-done = (bf16[320,3840]{1,0:T(8,128)(2,1)}, bf16[320,1280]{1,0:T(8,128)(2,1)}, bf16[320,1280]{1,0:T(8,128)(2,1)}, bf16[320,1280]{1,0:T(8,128)(2,1)}) async-done(((bf16[320,3840]{1,0:T(8,128)(2,1)}, bf16[320,1280]{1,0:T(8,128)(2,1)}, bf16[320,1280]{1,0:T(8,128)(2,1)}, bf16[320,1280]{1,0:T(8,128)(2,1)}), (bf16[320,3840]{1,0:T(8,128)(2,1)}, bf16[320,1280]{1,0:T(8,128)(2,1)}, ...) | async-done | bytes 4915216 | tf_op jit(solution)/shard_map/psum | solution.py:238
  1652.4 12.6 fusion.93
  (365 shorter events, 682.7 us)
Async XLA Ops:
  7.2 106.6 %all-gather.7.cloned.1.call-start = ((), (), s32[]{:S(2)}) async-start(), calls=%async_computation.6 | async-start | bytes 12288000 | tf_op jit(solution)/shard_map/all_gather | solution.py:87
  11.3 215.0 %all-gather.11.cloned.1.call-start = ((), (), s32[]{:S(2)}) async-start(), calls=%async_computation.8 | async-start | bytes 11796480 | tf_op jit(solution)/shard_map/all_gather | solution.py:110
  13.0 112.2 %copy-start.37 = (f32[512]{0:T(512)}, f32[512]{0:T(512)S(1)}, u32[]{:S(2)}) copy-start(f32[512]{0:T(512)S(1)} %add_rsqrt_fusion.1) | copy-start | bytes 6148
  13.6 111.5 %copy-start.30 = (f32[1280]{0:T(1024)}, f32[1280]{0:T(1024)S(1)}, u32[]{:S(2)}) copy-start(f32[1280]{0:T(1024)S(1)} %get-tuple-element.485) | copy-start | bytes 15364
  126.8 199.6 %all-gather.9.cloned.1.call-start = ((), (), s32[]{:S(2)}) async-start(), calls=%async_computation.7 | async-start | bytes 11796480 | tf_op jit(solution)/shard_map/all_gather | solution.py:111
  127.6 498.9 %all-gather.13.cloned.1.call-start = ((), (), s32[]{:S(2)}) async-start(), calls=%async_computation.9 | async-start | bytes 4096000 | tf_op jit(solution)/shard_map/all_gather | solution.py:88
  129.2 503.1 %all-gather.15.cloned.1.call-start = ((), (), s32[]{:S(2)}) async-start(), calls=%async_computation.10 | async-start | bytes 4096000 | tf_op jit(solution)/shard_map/all_gather | solution.py:89
  130.3 508.4 %all-gather.17.cloned.1.call-start = ((), (), s32[]{:S(2)}) async-start(), calls=%async_computation.11 | async-start | bytes 4096000 | tf_op jit(solution)/shard_map/all_gather | solution.py:90
  131.9 1050.0 %reduce-scatter.9.cloned.1.call-start = ((), (), s32[]{:S(2)}) async-start(), calls=%async_computation.13 | async-start | bytes 11796480 | tf_op jit(solution)/shard_map/reduce_scatter | solution.py:198
  132.6 5.3 copy-start.39
  626.4 5.9 copy-start.28
  632.3 14.2 copy-start.34
  632.3 6.3 copy-start.21
  638.7 5.1 copy-start.5
  638.7 5.1 copy-start.41
  1073.8 218.3 %reduce-scatter.7.cloned.1.call-start = ((), (), s32[]{:S(2)}) async-start(), calls=%async_computation.12 | async-start | bytes 11796480 | tf_op jit(solution)/shard_map/reduce_scatter | solution.py:195
  1074.5 264.5 %reduce-scatter.13.cloned.1.call-start = ((), (), s32[]{:S(2)}) async-start(), calls=%async_computation.15 | async-start | bytes 4096000 | tf_op jit(solution)/shard_map/reduce_scatter | solution.py:227
  1080.5 307.1 %reduce-scatter.15.cloned.1.call-start = ((), (), s32[]{:S(2)}) async-start(), calls=%async_computation.16 | async-start | bytes 4096000 | tf_op jit(solution)/shard_map/reduce_scatter | solution.py:230
  1087.2 349.0 %reduce-scatter.17.cloned.1.call-start = ((), (), s32[]{:S(2)}) async-start(), calls=%async_computation.17 | async-start | bytes 4096000 | tf_op jit(solution)/shard_map/reduce_scatter | solution.py:233
  1094.0 443.5 %reduce-scatter.11.cloned.1.call-start = ((), (), s32[]{:S(2)}) async-start(), calls=%async_computation.14 | async-start | bytes 12288000 | tf_op jit(solution)/shard_map/reduce_scatter | solution.py:224
  1099.1 192.9 %copy-start.3 = (bf16[1,512,1280]{2,1,0:T(8,128)(2,1)S(1)}, bf16[1,512,1280]{2,1,0:T(8,128)(2,1)}, u32[]{:S(2)}) copy-start(bf16[1,512,1280]{2,1,0:T(8,128)(2,1)} %param.24) | copy-start | bytes 3932164
  1099.1 192.9 %copy-start.31 = (f32[1280]{0:T(1024)S(1)}, f32[1280]{0:T(1024)}, u32[]{:S(2)}) copy-start(f32[1280]{0:T(1024)} %copy-done.30) | copy-start | bytes 15364
  1099.1 192.9 %copy-start.38 = (f32[512]{0:T(512)S(1)}, f32[512]{0:T(512)}, u32[]{:S(2)}) copy-start(f32[512]{0:T(512)} %copy-done.37) | copy-start | bytes 6148
  1301.8 350.6 %all-reduce.3.cloned.1.call-start = ((), (), s32[]{:S(2)}) async-start(), calls=%async_computation.18 | async-start | bytes 9830400 | tf_op jit(solution)/shard_map/psum | solution.py:238
  1537.5 10.9 copy-start.36
  1537.5 51.9 %copy-start.32 = (f32[2640]{0:T(1024)S(1)}, f32[2640]{0:T(1024)}, u32[]{:S(2)}) copy-start(f32[2640]{0:T(1024)} %param.40) | copy-start | bytes 31684
  1537.6 51.9 %copy-start.33 = (f32[2640]{0:T(1024)S(1)}, f32[2640]{0:T(1024)}, u32[]{:S(2)}) copy-start(f32[2640]{0:T(1024)} %param.41) | copy-start | bytes 31684
  1652.4 12.6 copy-start.10
  1652.4 12.6 copy-start.15
  1652.4 12.6 copy-start.16
  1652.4 13.0 copy-start.25
  1665.4 4.7 copy-start.24
  (25 other events, 60.5 us)
Sparse Core Ops, SparseCore 0:
  11.5 102.2 all-gather.6
  126.9 99.3 all-gather.10
  228.6 97.7 all-gather.8
  328.7 43.4 all-gather.12
  374.4 45.0 all-gather.14
  421.8 45.0 all-gather.16
  1073.9 107.9 reduce-scatter.8
  1184.2 107.7 reduce-scatter.6
  1295.6 43.3 reduce-scatter.12
  1342.5 45.0 reduce-scatter.14
  1391.2 45.0 reduce-scatter.16
  1439.2 98.2 reduce-scatter.10
  1540.1 112.2 all-reduce.2
where the time goes:
time: 1690 us; the launch traced here: 1680 us
  waiting for transfers between devices  705 us (42%)
  matrix products  582 us (34%)
  local copies, waits for them, and re-layouts  208 us (12%)
  other arithmetic  132 us (8%)
  blocking collectives  41 us (2%)
    dot_general x16, matrix products, head_scores(): jnp.einsum('qhd,khd->hqk', query_heads, key_heads, preferred_element_type...  152 us
    reduce_scatter x1, waiting for transfers between devices, body(): lax.psum_scatter(dkeys_all.astype(jnp.bfloat16), 'ctx', scatter_dimension...  110 us
    reduce_scatter x1, waiting for transfers between devices, body(): lax.psum_scatter(grad_qkv.astype(jnp.bfloat16), 'fsdp', scatter_dimension...  101 us
    all_gather x1, waiting for transfers between devices, body(): lax.all_gather(w_qkv.astype(bf16), 'fsdp', axis=0, tiled=True)  100 us
    dot_general x8, matrix products, back_step(): jnp.einsum('qhd,khd->hqk', dattn_heads, key_set[1], preferred_element_typ...  88.4 us
    all_gather x1, waiting for transfers between devices, body(): lax.all_gather(keys_here, 'ctx', axis=0, tiled=True)  83.4 us
    reduce_scatter x1, waiting for transfers between devices, body(): lax.psum_scatter(dvalues_all.astype(jnp.bfloat16), 'ctx', scatter_dimensi...  81 us
    unnamed x97, local copies, waits for them, and re-layouts  81 us
  transfers between devices with their start and end apart: 13, of which 10 were waited for; matrix products, arithmetic and copies ran while one was open for 26% of the time, Pallas kernels for 0%

commit v1 on v0

--- a/solution.py
+++ b/solution.py
@@ -20,6 +20,18 @@
 small_rate = 0.75
 qkv_rate_base = 1.0
 scale_base = 1.442695
+
+
+def gather_by_bits(shard, axis, dim):
+    ways, here = (lax.axis_size(axis), lax.axis_index(axis))
+    grown, reach = (shard, 1)
+    while reach < ways:
+        theirs = lax.ppermute(grown, axis, [(d, d ^ reach) for d in range(ways)])
+        mine_first = jnp.concatenate([grown, theirs], axis=dim)
+        theirs_first = jnp.concatenate([theirs, grown], axis=dim)
+        grown = jnp.where(here & reach == 0, mine_first, theirs_first)
+        reach = 2 * reach
+    return grown
 
 
 def token_layout(block_ids):
@@ -108,7 +120,7 @@
     values_here = qkv[:, 2 * D :].astype(bf16)
     keys_all, values_all = (
         lax.all_gather(keys_here, "ctx", axis=0, tiled=True),
-        lax.all_gather(values_here, "ctx", axis=0, tiled=True),
+        gather_by_bits(values_here, "ctx", 0),
     )
     key_total = keys_all.shape[0]
     key_block = math.gcd(key_total, 512)

time: 1690 us -> 1950 us (1.15)
  waiting for transfers between devices: 705 us -> 938 us
  other arithmetic: 132 us -> 152 us
    ppermute x0 -> x3, waiting for transfers between devices: none -> 359 us  [gather_by_bits(): theirs = lax.ppermute(grown, axis, [(d, d ^ reach) for d in range(ways)])]
    all_gather x1, waiting for transfers between devices: 83.4 us -> 0.01 us  [body(): lax.all_gather(keys_here, 'ctx', axis=0, tiled=True)]
    all_gather x1 -> x0, waiting for transfers between devices: 42.4 us -> none  [body(): lax.all_gather(values_here, 'ctx', axis=0, tiled=True)]
    reshape x1 -> x0, local copies, waits for them, and re-layouts: 29.8 us -> none  [body(): values_all.reshape(num_blocks, key_block, H, HD)]
    select_n x0 -> x1, local copies, waits for them, and re-layouts: none -> 29.7 us  [gather_by_bits(): grown = jnp.where(here & reach == 0, mine_first, theirs_first)]
    select_n x0 -> x3, other arithmetic: none -> 20.9 us  [gather_by_bits(): grown = jnp.where(here & reach == 0, mine_first, theirs_first)]
    unnamed x97 -> x99, local copies, waits for them, and re-layouts: 81 us -> 80.4 us
  transfers between devices with their start and end apart: 13 -> 15, of which waited for: 10 -> 11; matrix products, arithmetic and copies ran while one was open for 26% -> 23% of each run, Pallas kernels for 0% -> 0%
where the time goes in v1:
time: 1950 us; the launch traced here: 1940 us
  waiting for transfers between devices  938 us (48%)
  matrix products  581 us (30%)
  local copies, waits for them, and re-layouts  207 us (11%)
  other arithmetic  152 us (8%)
  blocking collectives  41.1 us (2%)
    ppermute x3, waiting for transfers between devices, gather_by_bits(): theirs = lax.ppermute(grown, axis, [(d, d ^ reach) for d in range(ways)])  359 us
    dot_general x16, matrix products, head_scores(): jnp.einsum('qhd,khd->hqk', query_heads, key_heads, preferred_element_type...  152 us
    reduce_scatter x1, waiting for transfers between devices, body(): lax.psum_scatter(dkeys_all.astype(jnp.bfloat16), 'ctx', scatter_dimension...  110 us
    reduce_scatter x1, waiting for transfers between devices, body(): lax.psum_scatter(grad_qkv.astype(jnp.bfloat16), 'fsdp', scatter_dimension...  101 us
    all_gather x1, waiting for transfers between devices, body(): lax.all_gather(w_qkv.astype(bf16), 'fsdp', axis=0, tiled=True)  100 us
    dot_general x8, matrix products, back_step(): jnp.einsum('qhd,khd->hqk', dattn_heads, key_set[1], preferred_element_typ...  88.4 us
    reduce_scatter x1, waiting for transfers between devices, body(): lax.psum_scatter(dvalues_all.astype(jnp.bfloat16), 'ctx', scatter_dimensi...  81.4 us
    unnamed x99, local copies, waits for them, and re-layouts  80.4 us
  transfers between devices with their start and end apart: 15, of which 11 were waited for; matrix products, arithmetic and copies ran while one was open for 23% of the time, Pallas kernels for 0%

profile of v1, /device:TPU:0, one launch (start us, length us, event | category | flops | bytes accessed | tf_op | source)
XLA Modules:
  0.0 1938.3 jit_solution(16632629895353745991)
XLA Ops:
  13.6 100.2 %all-gather.6.cloned.1.call-done = bf16[1280,3840]{1,0:T(8,128)(2,1)} async-done(((bf16[320,3840]{1,0:T(8,128)(2,1)}), bf16[1280,3840]{1,0:T(8,128)(2,1)}) %all-gather.6.cloned.1.call-update) | async-done | bytes 9830416 | tf_op jit(solution)/shard_map/all_gather | solution.py:99
  113.8 11.3 fusion.97
  137.0 140.7 %collective-permute-done.1 = bf16[1024,1280]{1,0:T(8,128)(2,1)} collective-permute-done((bf16[1024,1280]{1,0:T(8,128)(2,1)S(1)}, bf16[1024,1280]{1,0:T(8,128)(2,1)}, u32[]{:S(2)}, u32[]{:S(2)}) %collective-permute-start.1) | collective-permute-done | bytes 2621472 | tf_op jit(solution)/shard_map/ppermute | solution.py:29
  295.4 215.2 %collective-permute-done.2 = bf16[2048,1280]{1,0:T(8,128)(2,1)} collective-permute-done((bf16[2048,1280]{1,0:T(8,128)(2,1)}, bf16[2048,1280]{1,0:T(8,128)(2,1)}, u32[]{:S(2)}, u32[]{:S(2)}) %collective-permute-start.2) | collective-permute-done | bytes 5242912 | tf_op jit(solution)/shard_map/ppermute | solution.py:29
  510.6 13.0 maximum_select_fusion
  523.6 29.7 %reshape.411 = bf16[8,512,16,80]{3,2,1,0:T(8,128)(2,1)} reshape(bf16[4096,1280]{1,0:T(8,128)(2,1)} %maximum_select_fusion) | data formatting | bytes 20971520 | tf_op jit(solution)/shard_map/jit(_where)/select_n | solution.py:32
  553.3 21.6 %copy.62 = bf16[8,512,16,80]{1,3,2,0:T(8,128)(2,1)} copy(bf16[8,512,16,80]{3,2,1,0:T(8,128)(2,1)} %reshape.411) | data formatting | bytes 20971520
  574.9 14.3 copy.59
  589.2 15.0 copy.93
  604.2 16.3 copy.63
  620.5 11.7 copy.61
  632.2 148.9 %while.39 = (s32[]{:T(128)}, f32[16,512]{1,0:T(8,128)S(1)}, f32[16,512]{1,0:T(8,128)S(1)}, s32[8,512]{1,0:T(8,128)S(1)}, s32[512]{0:T(512)S(1)}, /*index=5*/s32[...) while((s32[]{:T(128)}, f32[16,512]{1,0:T(8,128)S(1)}, ...), condition=%wide.region_4.5_spmd.clone, body=%wide.region_1.4_spmd.clone.sunk | while | flops 693150208 | bytes 37405832 | solution.py:147
  781.1 95.0 %while.40 = (s32[]{:T(128)}, f32[512,16,80]{0,2,1:T(8,128)}, bf16[8,512,16,80]{1,3,2,0:T(8,128)(2,1)}, s32[8,512]{1,0:T(8,128)S(1)}, s32[512]{0:T(512)S(1)}, /*i...) while((s32[]{:T(128)}, f32[512,16,80]{0,2,1:T(8,128)}, ...), condition=%wide.region_6.7_spmd.clone, body=%wide.region_5.6_spmd.clone.sunk | while | flops 1357120000 | bytes 13157527 | solution.py:160
  908.2 418.2 %while.41 = (s32[]{:T(128)}, f32[512,16,80]{0,2,1:T(8,128)}, bf16[8,512,1280]{2,1,0:T(8,128)(2,1)}, bf16[8,512,1280]{2,1,0:T(8,128)(2,1)}, bf16[8,512,16,80]{1,3...) while((s32[]{:T(128)}, f32[512,16,80]{0,2,1:T(8,128)}, ...), condition=%wide.region_11.12_spmd.clone, body=%wide.region_10.11_spmd.clone.sunk | while | flops 3391357440 | bytes 103924920 | solution.py:203
  918.1 11.1 fusion.157
  969.7 11.1 fusion.157
  1022.1 11.1 fusion.157
  1074.5 11.1 fusion.157
  1126.8 11.0 fusion.157
  1179.2 11.1 fusion.157
  1231.5 11.1 fusion.157
  1283.8 11.0 fusion.157
  1353.6 81.4 %reduce-scatter.9.cloned.1.call-done = bf16[512,1280]{1,0:T(8,128)(2,1)} async-done(((bf16[4096,1280]{1,0:T(8,128)(2,1)}), bf16[512,1280]{1,0:T(8,128)(2,1)}) %reduce-scatter.9.cloned.1.call-update) | async-done | bytes 1310736 | tf_op jit(solution)/shard_map/reduce_scatter | solution.py:210
  1435.1 110.1 %reduce-scatter.7.cloned.1.call-done = bf16[512,1280]{1,0:T(8,128)(2,1)} async-done(((bf16[4096,1280]{1,0:T(8,128)(2,1)}), bf16[512,1280]{1,0:T(8,128)(2,1)}) %reduce-scatter.7.cloned.1.call-update) | async-done | bytes 1310736 | tf_op jit(solution)/shard_map/reduce_scatter | solution.py:207
  1562.4 29.8 %reduce-scatter.13.cloned.1.call-done = bf16[320,1280]{1,0:T(8,128)(2,1)} async-done(((bf16[1280,1280]{1,0:T(8,128)(2,1)}), bf16[320,1280]{1,0:T(8,128)(2,1)}) %reduce-scatter.13.cloned.1.call-update) | async-done | bytes 819216 | tf_op jit(solution)/shard_map/reduce_scatter | solution.py:239
  1592.2 48.7 %reduce-scatter.15.cloned.1.call-done = bf16[320,1280]{1,0:T(8,128)(2,1)} async-done(((bf16[1280,1280]{1,0:T(8,128)(2,1)}), bf16[320,1280]{1,0:T(8,128)(2,1)}) %reduce-scatter.15.cloned.1.call-update) | async-done | bytes 819216 | tf_op jit(solution)/shard_map/reduce_scatter | solution.py:242
  1640.9 48.5 %reduce-scatter.17.cloned.1.call-done = bf16[320,1280]{1,0:T(8,128)(2,1)} async-done(((bf16[1280,1280]{1,0:T(8,128)(2,1)}), bf16[320,1280]{1,0:T(8,128)(2,1)}) %reduce-scatter.17.cloned.1.call-update) | async-done | bytes 819216 | tf_op jit(solution)/shard_map/reduce_scatter | solution.py:245
  1689.4 101.4 %reduce-scatter.11.cloned.1.call-done = bf16[320,3840]{1,0:T(8,128)(2,1)} async-done(((bf16[1280,3840]{1,0:T(8,128)(2,1)}), bf16[320,3840]{1,0:T(8,128)(2,1)}) %reduce-scatter.11.cloned.1.call-update) | async-done | bytes 2457616 | tf_op jit(solution)/shard_map/reduce_scatter | solution.py:236
  1790.9 10.9 fusion.56
  1801.8 41.1 %psum.39 = f32[2640]{0:T(1024)S(1)} all-reduce(f32[2640]{0:T(1024)S(1)} %pad_maximum_fusion.3), channel_id=1, replica_groups=mesh['ctx'=8,'fsdp'=4] {'ctx','fsdp'}, use_global_device_ids=true, to_apply=%region_26.27 | all-reduce | flops 2640 | bytes 21120 | tf_op jit(solution)/shard_map/psum | solution.py:230
  1847.9 57.7 %all-reduce.3.cloned.1.call-done = (bf16[320,3840]{1,0:T(8,128)(2,1)}, bf16[320,1280]{1,0:T(8,128)(2,1)}, bf16[320,1280]{1,0:T(8,128)(2,1)}, bf16[320,1280]{1,0:T(8,128)(2,1)}) async-done(((bf16[320,3840]{1,0:T(8,128)(2,1)}, bf16[320,1280]{1,0:T(8,128)(2,1)}, bf16[320,1280]{1,0:T(8,128)(2,1)}, bf16[320,1280]{1,0:T(8,128)(2,1)}), (bf16[320,3840]{1,0:T(8,128)(2,1)}, bf16[320,1280]{1,0:T(8,128)(2,1)}, ...) | async-done | bytes 4915216 | tf_op jit(solution)/shard_map/psum | solution.py:250
  1905.6 12.6 fusion.93
  (373 shorter events, 702.9 us)
Async XLA Ops:
  7.2 106.6 %all-gather.6.cloned.1.call-start = ((), (), s32[]{:S(2)}) async-start(), calls=%async_computation.6 | async-start | bytes 12288000 | tf_op jit(solution)/shard_map/all_gather | solution.py:99
  11.3 563.6 %all-gather.8.cloned.1.call-start = ((), (), s32[]{:S(2)}) async-start(), calls=%async_computation.7 | async-start | bytes 11796480 | tf_op jit(solution)/shard_map/all_gather | solution.py:122
  13.0 112.2 %copy-start.38 = (f32[512]{0:T(512)}, f32[512]{0:T(512)S(1)}, u32[]{:S(2)}) copy-start(f32[512]{0:T(512)S(1)} %add_rsqrt_fusion.1) | copy-start | bytes 6148
  13.6 111.6 %copy-start.31 = (f32[1280]{0:T(1024)}, f32[1280]{0:T(1024)S(1)}, u32[]{:S(2)}) copy-start(f32[1280]{0:T(1024)S(1)} %get-tuple-element.485) | copy-start | bytes 15364
  126.4 752.8 %all-gather.10.cloned.1.call-start = ((), (), s32[]{:S(2)}) async-start(), calls=%async_computation.8 | async-start | bytes 4096000 | tf_op jit(solution)/shard_map/all_gather | solution.py:100
  128.1 757.0 %all-gather.12.cloned.1.call-start = ((), (), s32[]{:S(2)}) async-start(), calls=%async_computation.9 | async-start | bytes 4096000 | tf_op jit(solution)/shard_map/all_gather | solution.py:101
  128.1 3.2 collective-permute-start
  128.2 7.8 copy-start.11
  134.5 143.3 %collective-permute-start.1 = (bf16[1024,1280]{1,0:T(8,128)(2,1)S(1)}, bf16[1024,1280]{1,0:T(8,128)(2,1)}, u32[]{:S(2)}, u32[]{:S(2)}) collective-permute-start(bf16[1024,1280]{1,0:T(8,128)(2,1)S(1)} %maximum_select_fusion.2), channel_id=1, source_target_pairs={{0,8},{4,12},{8,0},{12,4},{16,24},{20,28},{24,16},{28,20},{1,9},{5... | collective-permute-start | bytes 7864328 | tf_op jit(solution)/shard_map/ppermute | solution.py:29
  137.0 754.5 %all-gather.14.cloned.1.call-start = ((), (), s32[]{:S(2)}) async-start(), calls=%async_computation.10 | async-start | bytes 4096000 | tf_op jit(solution)/shard_map/all_gather | solution.py:102
  137.0 146.5 %copy-start.13 = (f32[320,1280]{1,0:T(8,128)S(1)}, f32[320,1280]{1,0:T(8,128)}, u32[]{:S(2)}) copy-start(f32[320,1280]{1,0:T(8,128)} %param.36) | copy-start | bytes 4915204
  282.5 228.0 %collective-permute-start.2 = (bf16[2048,1280]{1,0:T(8,128)(2,1)}, bf16[2048,1280]{1,0:T(8,128)(2,1)}, u32[]{:S(2)}, u32[]{:S(2)}) collective-permute-start(bf16[2048,1280]{1,0:T(8,128)(2,1)} %maximum_select_fusion.1), channel_id=1, source_target_pairs={{0,16},{4,20},{8,24},{12,28},{16,0},{20,4},{24,8},{28,12},{1,17},{... | collective-permute-start | bytes 15728648 | tf_op jit(solution)/shard_map/ppermute | solution.py:29
  284.5 1150.5 %reduce-scatter.9.cloned.1.call-start = ((), (), s32[]{:S(2)}) async-start(), calls=%async_computation.12 | async-start | bytes 11796480 | tf_op jit(solution)/shard_map/reduce_scatter | solution.py:210
  879.2 5.9 copy-start.29
  885.1 14.2 copy-start.35
  885.1 6.3 copy-start.22
  1326.5 218.7 %reduce-scatter.7.cloned.1.call-start = ((), (), s32[]{:S(2)}) async-start(), calls=%async_computation.11 | async-start | bytes 11796480 | tf_op jit(solution)/shard_map/reduce_scatter | solution.py:207
  1327.2 265.0 %reduce-scatter.13.cloned.1.call-start = ((), (), s32[]{:S(2)}) async-start(), calls=%async_computation.14 | async-start | bytes 4096000 | tf_op jit(solution)/shard_map/reduce_scatter | solution.py:239
  1333.2 307.7 %reduce-scatter.15.cloned.1.call-start = ((), (), s32[]{:S(2)}) async-start(), calls=%async_computation.15 | async-start | bytes 4096000 | tf_op jit(solution)/shard_map/reduce_scatter | solution.py:242
  1340.0 349.5 %reduce-scatter.17.cloned.1.call-start = ((), (), s32[]{:S(2)}) async-start(), calls=%async_computation.16 | async-start | bytes 4096000 | tf_op jit(solution)/shard_map/reduce_scatter | solution.py:245
  1346.7 444.1 %reduce-scatter.11.cloned.1.call-start = ((), (), s32[]{:S(2)}) async-start(), calls=%async_computation.13 | async-start | bytes 12288000 | tf_op jit(solution)/shard_map/reduce_scatter | solution.py:236
  1351.9 193.3 %copy-start.3 = (bf16[1,512,1280]{2,1,0:T(8,128)(2,1)S(1)}, bf16[1,512,1280]{2,1,0:T(8,128)(2,1)}, u32[]{:S(2)}) copy-start(bf16[1,512,1280]{2,1,0:T(8,128)(2,1)} %param.24) | copy-start | bytes 3932164
  1351.9 193.3 %copy-start.32 = (f32[1280]{0:T(1024)S(1)}, f32[1280]{0:T(1024)}, u32[]{:S(2)}) copy-start(f32[1280]{0:T(1024)} %copy-done.31) | copy-start | bytes 15364
  1351.9 193.2 %copy-start.39 = (f32[512]{0:T(512)S(1)}, f32[512]{0:T(512)}, u32[]{:S(2)}) copy-start(f32[512]{0:T(512)} %copy-done.38) | copy-start | bytes 6148
  1554.9 350.6 %all-reduce.3.cloned.1.call-start = ((), (), s32[]{:S(2)}) async-start(), calls=%async_computation.17 | async-start | bytes 9830400 | tf_op jit(solution)/shard_map/psum | solution.py:250
  1790.8 10.9 copy-start.37
  1790.9 52.0 %copy-start.33 = (f32[2640]{0:T(1024)S(1)}, f32[2640]{0:T(1024)}, u32[]{:S(2)}) copy-start(f32[2640]{0:T(1024)} %param.40) | copy-start | bytes 31684
  1790.9 52.0 %copy-start.34 = (f32[2640]{0:T(1024)S(1)}, f32[2640]{0:T(1024)}, u32[]{:S(2)}) copy-start(f32[2640]{0:T(1024)} %param.41) | copy-start | bytes 31684
  1905.5 12.6 copy-start.10
  1905.6 12.6 copy-start.16
  1905.6 12.6 copy-start.17
  1905.6 13.0 copy-start.26
  (28 other events, 78.4 us)
Sparse Core Ops, SparseCore 0:
  11.5 102.2 all-gather.5
  126.5 149.7 all-gather.7
  278.7 47.2 all-gather.9
  328.3 45.0 all-gather.11
  375.6 45.0 all-gather.13
  1326.6 108.4 reduce-scatter.8
  1437.4 107.7 reduce-scatter.6
  1548.7 43.4 reduce-scatter.12
  1595.8 45.0 reduce-scatter.14
  1644.3 45.0 reduce-scatter.16
  1692.6 98.2 reduce-scatter.10
  1793.3 112.2 all-reduce.2
